TPU v7x, 32 devices: a whole 2x2x4 slice. The times are simulated.
32 devices in a mesh: seq: 8 (over y, x, core), exp: 4 (over z).
Axes of the slice: x: 2, y: 2, z: 4, core: 2. Of those that a mesh axis runs over, the one named last changes fastest.
Arguments:
- mixer_input: bfloat16 [512, 8192], P('seq', 'exp'), may hold values from -6 to 6
- gate_input: bfloat16 [512, 8192], P('seq', 'exp'), may hold values from -6 to 6
- delta_raw: bfloat16 [512, 8192], P('seq', 'exp'), may hold values from -7 to 2051
- input_coef: bfloat16 [512, 16], P('seq'), may hold values from 0.19921875 to 1.796875
- output_coef: bfloat16 [512, 16], P('seq'), may hold values from -3 to 3
- decay_rate: float32 [16, 8192], P(None, 'exp'), may hold values from 3.90625e-05 to 0.05
- conv_weight: float32 [4, 8192], P(None, 'exp'), may hold values from -3 to 3
- conv_bias: float32 [8192], P('exp'), may hold values from -3 to 3
- skip_gain: float32 [8192], P('exp'), may hold values from 0.5 to 1.5
- out_weight: bfloat16 [8192, 4096], P('exp', 'seq'), may hold values from -0.0625 to 0.0625
- residual: bfloat16 [512, 4096], P(('seq', 'exp')), may hold values from -6 to 6
- norm_gain: float32 [4096], replicated, may hold values from 0.1 to 1.9
- router_weight: bfloat16 [4096, 4], replicated, may hold values from -0.09375 to 0.09375
- expert_ids: int32 [512, 2], P(('seq', 'exp')), may hold values from 0 to 3, all different within a row; in each aligned block of 16 rows (0 to 15, 16 to 31, ...) at most 9 rows name the same one
- gate_weight: bfloat16 [4, 4096, 12288], P('exp', None, 'seq'), may hold values from -0.09375 to 0.09375
- up_weight: bfloat16 [4, 4096, 12288], P('exp', None, 'seq'), may hold values from -0.09375 to 0.09375
- down_weight: bfloat16 [4, 12288, 4096], P('exp', 'seq'), may hold values from -0.0546875 to 0.0546875
Outputs:
- mixed: bfloat16 [512, 8192], P('seq', 'exp')
- final: bfloat16 [512, 4096], P(('seq', 'exp'))
Inputs may be any that keep to these rules, and one draw needn't show every extreme that they name: `expert_ids`: each row names two different experts. In each aligned block of 16 rows (the rows of one device) no expert is named by more than 9 rows, and in some block one expert is named by exactly 9 rows.
All inputs are finite; a program needn't handle non-finite values.
Results may differ from a plain program's by a relative error of at most 0.015.
Values may be sent and summed in bfloat16 or wider, within the bound.
A program may use at most 128 MiB of HBM per device.

v0:
```python
import jax
import jax.numpy as jnp
from jax import lax
from jax.sharding import PartitionSpec as P

KCONV = 4


def from_behind(block, axis, distance):
    devices = range(lax.axis_size(axis))
    route = [(i - distance, i) for i in devices if i - distance in devices]
    return lax.ppermute(block, axis, route)


def carried_in(part, axis, combine, identity):
    place = lax.axis_index(axis)
    gathered = jax.tree.map(lambda a: lax.all_gather(a, axis), part)
    state = jax.tree.map(lambda a, e: jnp.zeros_like(a) + jnp.asarray(e, a.dtype), part, identity)

    def one(turn, state):
        return combine(
            state, jax.tree.map(lambda a: lax.dynamic_index_in_dim(a, turn, 0, False), gathered)
        )

    return lax.fori_loop(0, place, one, state)


def sweep(state, delta, convolved, input_rows, output_rows, decay_rate):

    def advance(carry, inputs):
        delta_row, value_row, input_row, output_row = inputs
        retain = jnp.exp(-delta_row[None, :] * decay_rate)
        carry = retain * carry + (1.0 - retain) * input_row[:, None] * value_row[None, :]
        return (carry, jnp.sum(output_row[:, None] * carry, axis=0))

    return lax.scan(advance, state, (delta, convolved, input_rows, output_rows), unroll=8)


def chain(earlier, later):
    return (earlier[0] * later[0], later[0] * earlier[1] + later[1])


def shards(
    mixer_input,
    gate_input,
    delta_raw,
    input_coef,
    output_coef,
    decay_rate,
    conv_weight,
    conv_bias,
    skip_gain,
    out_weight,
    residual,
    norm_gain,
    router_weight,
    expert_ids,
    gate_weight,
    up_weight,
    down_weight,
):
    length = mixer_input.shape[0]
    width = mixer_input.shape[1]
    tail = mixer_input[length - (KCONV - 1) :]
    before = from_behind(tail, "seq", 1)
    padded = jnp.concatenate([before, mixer_input], axis=0).astype(jnp.float32)
    summed = jnp.broadcast_to(conv_bias[None, :], (length, width))
    for offset in range(KCONV):
        summed = summed + conv_weight[offset][None, :] * padded[offset : offset + length]
    convolved = jax.nn.silu(summed)
    delta = jax.nn.softplus(delta_raw.astype(jnp.float32))
    input_rows = input_coef.astype(jnp.float32)
    output_rows = output_coef.astype(jnp.float32)
    zero_state = jnp.zeros(decay_rate.shape, jnp.float32)
    end_state, local_out = sweep(zero_state, delta, convolved, input_rows, output_rows, decay_rate)
    block_decay = jnp.exp(-jnp.sum(delta, axis=0)[None, :] * decay_rate)
    carried_decay, start_state = carried_in(
        (block_decay, end_state), "seq", chain, (jnp.ones_like(block_decay), zero_state)
    )
    last_state, scan_out = sweep(start_state, delta, convolved, input_rows, output_rows, decay_rate)
    mixed = (
        (scan_out + skip_gain[None, :] * convolved) * jax.nn.silu(gate_input.astype(jnp.float32))
    ).astype(jnp.bfloat16)
    rows = residual.shape[0]
    model_width = residual.shape[1]
    full_weight = lax.all_gather(out_weight, "seq", axis=1, tiled=True)
    projected = lax.psum_scatter(
        jnp.dot(mixed, full_weight, preferred_element_type=jnp.float32).astype(jnp.bfloat16),
        "exp",
        scatter_dimension=0,
        tiled=True,
    ).astype(jnp.float32)
    hidden_state = residual.astype(jnp.float32) + projected
    scale = lax.rsqrt(jnp.mean(hidden_state * hidden_state, axis=1, keepdims=True) + 1e-06)
    normed = (hidden_state * scale * norm_gain[None, :]).astype(jnp.bfloat16)
    experts = router_weight.shape[1]
    capacity = 2 * rows // experts + 1
    logits = jnp.dot(normed, router_weight, preferred_element_type=jnp.float32)
    expert_range = jnp.arange(experts, dtype=jnp.int32)
    matches = expert_ids[:, :, None] == expert_range[None, None, :]
    chosen = jnp.sum(jnp.where(matches, logits[:, None, :], 0.0), axis=2)
    first = jax.nn.sigmoid(chosen[:, 0] - chosen[:, 1])
    flat_ids = expert_ids.reshape(-1)
    onehot = (flat_ids[:, None] == expert_range[None, :]).astype(jnp.int32)
    rank = jnp.sum((jnp.cumsum(onehot, axis=0) - onehot) * onehot, axis=1)
    target = flat_ids * capacity + rank
    placing = (jnp.arange(experts * capacity, dtype=jnp.int32)[:, None] == target[None, :]).astype(
        jnp.bfloat16
    )
    repeated = jnp.broadcast_to(normed[:, None, :], (rows, 2, model_width)).reshape(-1, model_width)
    outgoing = (
        jnp.dot(placing, repeated, preferred_element_type=jnp.float32)
        .astype(jnp.bfloat16)
        .reshape(experts, capacity, model_width)
    )
    arrived = lax.all_to_all(outgoing, "exp", split_axis=0, concat_axis=0, tiled=True)
    flat_rows = arrived.reshape(-1, arrived.shape[2])
    piece = lax.all_gather(flat_rows, "seq", axis=0, tiled=True)
    gating = jnp.dot(piece, gate_weight[0], preferred_element_type=jnp.float32)
    upward = jnp.dot(piece, up_weight[0], preferred_element_type=jnp.float32)
    activated = (jax.nn.silu(gating) * upward).astype(jnp.bfloat16)
    partial_out = jnp.dot(activated, down_weight[0], preferred_element_type=jnp.float32)
    summed_out = lax.psum_scatter(
        partial_out.astype(jnp.bfloat16), "seq", scatter_dimension=0, tiled=True
    )
    returned = lax.all_to_all(
        summed_out.reshape(arrived.shape), "exp", split_axis=0, concat_axis=0, tiled=True
    )
    flat_returned = returned.reshape(-1, model_width)
    picked = jnp.einsum(
        "sa,sd->ad", placing, flat_returned, preferred_element_type=jnp.float32
    ).reshape(rows, 2, model_width)
    moe_out = first[:, None] * picked[:, 0] + (1.0 - first)[:, None] * picked[:, 1]
    final = (hidden_state + moe_out).astype(jnp.bfloat16)
    return (mixed, final)


def solution(mesh):
    return jax.shard_map(
        shards,
        mesh=mesh,
        in_specs=(
            P("seq", "exp"),
            P("seq", "exp"),
            P("seq", "exp"),
            P("seq", None),
            P("seq", None),
            P(None, "exp"),
            P(None, "exp"),
            P("exp"),
            P("exp"),
            P("exp", "seq"),
            P(("seq", "exp"), None),
            P(),
            P(),
            P(("seq", "exp"), None),
            P("exp", None, "seq"),
            P("exp", None, "seq"),
            P("exp", "seq", None),
        ),
        out_specs=(P("seq", "exp"), P(("seq", "exp"), None)),
        check_vma=False,
    )
```

profile of v0, /device:TPU:0, one launch (start us, length us, event | category | flops | bytes accessed | tf_op | source)
XLA Modules:
  0.0 336.7 jit_solution(5825513231245469339)
XLA Ops:
  7.2 0.8 slice.264
  8.0 2.5 collective-permute-start
  10.5 1.3 fusion.46
  11.8 1.6 multiply_exponential_fusion
  13.5 0.9 fusion.58
  14.4 0.8 copy.36
  15.2 1.0 maximum_convert_fusion
  16.2 1.0 fusion.68
  17.3 4.0 %while.37 = (s32[]{:T(128)}, f32[16,2048]{1,0:T(8,128)S(1)}, f32[8,8,2048]{2,1,0:T(8,128)S(1)}, f32[16,2048]{1,0:T(8,128)S(1)}, f32[8,8,16]{2,1,0:T(8,128)S(1)},...) while((s32[]{:T(128)}, f32[16,2048]{1,0:T(8,128)S(1)}, ...), condition=%wide.region_2.3_spmd.clone, body=%wide.region_1.2_spmd.clone.sunk | while | flops 1622026 | bytes 789263 | solution.py:36
  21.3 0.6 copy-done.2
  22.1 0.7 all-gather.8.cloned.1.call-update
  22.9 16.7 %all-gather.10.cloned.1.call-done = f32[128,2048]{1,0:T(8,128)} async-done(((f32[16,2048]{1,0:T(8,128)}), f32[128,2048]{1,0:T(8,128)}) %all-gather.10.cloned.1.call-update) | async-done | bytes 1048592 | tf_op jit(solution)/shard_map/all_gather | solution.py:17
  39.6 26.0 %all-gather.12.cloned.1.call-done = f32[128,2048]{1,0:T(8,128)} async-done(((f32[16,2048]{1,0:T(8,128)}), f32[128,2048]{1,0:T(8,128)}) %all-gather.12.cloned.1.call-update) | async-done | bytes 1048592 | tf_op jit(solution)/shard_map/all_gather | solution.py:17
  65.7 9.4 %while.36 = (s32[]{:T(128)}, f32[16,2048]{1,0:T(8,128)S(1)}, f32[8,8,2048]{2,1,0:T(8,128)S(1)}, f32[8,8,2048]{2,1,0:T(8,128)S(1)}, f32[16,2048]{1,0:T(8,128)S(1)...) while((s32[]{:T(128)}, f32[16,2048]{1,0:T(8,128)S(1)}, ...), condition=%wide.region_14.15_spmd, body=%wide.region_5.14_spmd.sunk | while | flops 2883593 | bytes 2627097 | solution.py:36
  65.9 0.4 multiply_reduce_fusion.12
  66.4 0.3 multiply_reduce_fusion.13
  67.1 0.4 multiply_reduce_fusion.12
  67.5 0.3 multiply_reduce_fusion.13
  68.2 0.4 multiply_reduce_fusion.12
  69.4 0.4 multiply_reduce_fusion.12
  69.9 0.3 multiply_reduce_fusion.13
  70.6 0.4 multiply_reduce_fusion.12
  71.8 0.4 multiply_reduce_fusion.12
  72.2 0.3 multiply_reduce_fusion.13
  72.9 0.4 multiply_reduce_fusion.12
  73.4 0.3 multiply_reduce_fusion.13
  74.1 0.4 multiply_reduce_fusion.12
  74.6 0.3 multiply_reduce_fusion.13
  75.1 0.5 fusion.45
  75.7 85.0 %all-gather.8.cloned.1.call-done = bf16[2048,4096]{1,0:T(8,128)(2,1)} async-done(((bf16[2048,512]{1,0:T(8,128)(2,1)}), bf16[2048,4096]{1,0:T(8,128)(2,1)}) %all-gather.8.cloned.1.call-update) | async-done | bytes 16777232 | tf_op jit(solution)/shard_map/all_gather | solution.py:86
  160.6 9.6 %convolution_convert_fusion = bf16[64,4096]{1,0:T(8,128)(2,1)} fusion(bf16[64,2048]{1,0:T(8,128)(2,1)S(1)} %fusion.45, bf16[2048,4096]{1,0:T(8,128)(2,1)} %all-gather.8.cloned.1.call-done), kind=kOutput, calls=%fused_computation.101 | convolution fusion | flops 1074003968 | bytes 17563648 | tf_op jit(solution)/shard_map/dot_general | solution.py:88
  170.8 21.2 %reduce-scatter.4.cloned.1.call-done = bf16[16,4096]{1,0:T(8,128)(2,1)} async-done(((bf16[64,4096]{1,0:T(8,128)(2,1)}), bf16[16,4096]{1,0:T(8,128)(2,1)}) %reduce-scatter.4.cloned.1.call-update) | async-done | bytes 131088 | tf_op jit(solution)/shard_map/reduce_scatter | solution.py:87
  192.0 1.1 multiply_reduce_fusion.8
  193.1 1.0 multiply_convert_fusion
  194.8 15.5 %all_to_all.10 = bf16[4,9,4096]{2,1,0:T(8,128)(2,1)S(1)} all-to-all(bf16[4,9,4096]{2,1,0:T(8,128)(2,1)S(1)} %reshape.356), channel_id=1, replica_groups=mesh['seq'=8,'exp'=4] {'exp'}, dimensions={0} | all-to-all | bytes 589824 | tf_op jit(solution)/shard_map/all_to_all | solution.py:116
  210.3 0.8 reshape.366
  211.1 29.3 %all-gather.14.cloned.1.call-done = bf16[8,36,4096]{2,1,0:T(8,128)(2,1)} async-done(((bf16[1,36,4096]{2,1,0:T(8,128)(2,1)}), bf16[8,36,4096]{2,1,0:T(8,128)(2,1)}) %all-gather.14.cloned.1.call-update) | async-done | bytes 2359312 | tf_op jit(solution)/shard_map/all_gather | solution.py:118
  240.4 4.1 %reshape.367 = bf16[288,4096]{1,0:T(8,128)(2,1)} reshape(bf16[8,36,4096]{2,1,0:T(8,128)(2,1)} %all-gather.14.cloned.1.call-done) | data formatting | bytes 4718592
  244.5 10.4 %fusion.20 = f32[288,1536]{1,0:T(8,128)} fusion(bf16[288,4096]{1,0:T(8,128)(2,1)} %reshape.367, bf16[1,4096,1536]{2,1,0:T(8,128)(2,1)} %param.37), kind=kOutput, calls=%fused_computation.98 | convolution fusion | flops 3623878656 | bytes 16711680 | tf_op jit(solution)/shard_map/dot_general | solution.py:119
  254.9 18.3 %fusion.22 = bf16[288,4096]{1,0:T(8,128)(2,1)} fusion(bf16[1,1536,4096]{2,1,0:T(8,128)(2,1)} %param.39, bf16[288,4096]{1,0:T(8,128)(2,1)} %reshape.367, bf16[1,4096,1536]{2,1,0:T(8,128)(2,1)} %param.38, f32[288,1536]{1,0:T(8,128)} %fusion.20), kind=kOutput, calls=%fused_computation.100 | convolution fusion | flops 7251591168 | bytes 31653888 | tf_op jit(solution)/shard_map/dot_general | solution.py:122
  273.2 32.1 %fusion = bf16[40,4096]{1,0:T(8,128)(2,1)S(1)} fusion(bf16[288,4096]{1,0:T(8,128)(2,1)} %fusion.22), kind=kCustom, calls=%all-reduce-scatter | all-reduce-scatter fusion | flops 1310721 | bytes 2687488
  305.4 1.3 collective-permute-start.1
  306.8 0.6 dynamic-slice.36
  308.1 0.5 concatenate.7
  308.7 0.9 reshape.358
  309.6 4.6 %all-to-all-start.1 = ((bf16[4,9,4096]{2,1,0:T(8,128)(2,1)}), bf16[4,9,4096]{2,1,0:T(8,128)(2,1)S(1)}, u32[]{:S(2)}, u32[]{:S(2)}) async-start(bf16[4,9,4096]{2,1,0:T(8,128)(2,1)} %reshape.358), calls=%async_computation.2 | async-start | bytes 1048576 | tf_op jit(solution)/shard_map/all_to_all | solution.py:126
  314.4 14.7 %all-to-all-done.1 = bf16[4,9,4096]{2,1,0:T(8,128)(2,1)S(1)} async-done(((bf16[4,9,4096]{2,1,0:T(8,128)(2,1)}), bf16[4,9,4096]{2,1,0:T(8,128)(2,1)S(1)}, u32[]{:S(2)}, u32[]{:S(2)}) %all-to-all-start.1) | async-done | bytes 294944 | tf_op jit(solution)/shard_map/all_to_all | solution.py:126
  329.4 0.8 fusion.51
  (160 shorter events, 10.0 us)
Async XLA Ops:
  7.2 307.0 %copy-start = (bf16[4096,4]{0,1:T(4,128)(2,1)S(1)}, bf16[4096,4]{0,1:T(4,128)(2,1)}, u32[]{:S(2)}) copy-start(bf16[4096,4]{0,1:T(4,128)(2,1)} %param.35) | copy-start | bytes 98308
  7.2 32.5 %all-gather.10.cloned.1.call-start = ((), (), s32[]{:S(2)}) async-start(), calls=%async_computation.5 | async-start | bytes 1179648 | tf_op jit(solution)/shard_map/all_gather | solution.py:17
  8.0 9.3 %copy-start.1 = (f32[16,2048]{1,0:T(8,128)S(1)}, f32[16,2048]{1,0:T(8,128)}, u32[]{:S(2)}) copy-start(f32[16,2048]{1,0:T(8,128)} %param.28) | copy-start | bytes 393220
  8.0 7.2 %collective-permute-start = (bf16[3,2048]{1,0:T(4,128)(2,1)S(1)}, bf16[3,2048]{1,0:T(4,128)(2,1)S(1)}, u32[]{:S(2)}, u32[]{:S(2)}) collective-permute-start(bf16[3,2048]{1,0:T(4,128)(2,1)S(1)} %slice.264), channel_id=1, source_target_pairs={{0,4},{4,8},{8,12},{12,16},{16,20},{20,24},{24,28},{1,5},{5,9},{9,... | collective-permute-start | bytes 36872 | tf_op jit(solution)/shard_map/ppermute | solution.py:12
  13.4 52.2 %all-gather.12.cloned.1.call-start = ((), (), s32[]{:S(2)}) async-start(), calls=%async_computation.6 | async-start | bytes 1179648 | tf_op jit(solution)/shard_map/all_gather | solution.py:17
  17.3 5.5 %copy-start.10 = (bf16[64,16]{0,1:T(8,128)(2,1)S(1)}, bf16[64,16]{0,1:T(8,128)(2,1)}, u32[]{:S(2)}) copy-start(bf16[64,16]{0,1:T(8,128)(2,1)} %param.27) | copy-start | bytes 6148
  21.3 0.7 copy-start.2
  22.0 138.6 %all-gather.8.cloned.1.call-start = ((), (), s32[]{:S(2)}) async-start(), calls=%async_computation.3 | async-start | bytes 18874368 | tf_op jit(solution)/shard_map/all_gather | solution.py:86
  22.8 169.3 %reduce-scatter.4.cloned.1.call-start = ((), (), s32[]{:S(2)}) async-start(), calls=%async_computation.4 | async-start | bytes 655360 | tf_op jit(solution)/shard_map/reduce_scatter | solution.py:87
  65.6 9.5 %copy-start.6 = (bf16[64,2048]{1,0:T(8,128)(2,1)S(1)}, bf16[64,2048]{1,0:T(8,128)(2,1)}, u32[]{:S(2)}) copy-start(bf16[64,2048]{1,0:T(8,128)(2,1)} %param.24) | copy-start | bytes 786436
  65.7 9.4 %copy-start.7 = (f32[2048]{0:T(1024)S(1)}, f32[2048]{0:T(1024)}, u32[]{:S(2)}) copy-start(f32[2048]{0:T(1024)} %param.30) | copy-start | bytes 24580
  65.7 9.4 %copy-start.9 = (f32[2048]{0:T(1024)S(1)}, f32[2048]{0:T(1024)}, u32[]{:S(2)}) copy-start(f32[2048]{0:T(1024)} %param.31) | copy-start | bytes 24580
  75.6 94.6 %copy-start.3 = (bf16[64,2048]{1,0:T(8,128)(2,1)}, bf16[64,2048]{1,0:T(8,128)(2,1)S(1)}, u32[]{:S(2)}) copy-start(bf16[64,2048]{1,0:T(8,128)(2,1)S(1)} %fusion.45) | copy-start | bytes 786436
  75.6 94.7 %copy-start.11 = (s32[16,2]{0,1:T(2,128)S(1)}, s32[16,2]{0,1:T(2,128)}, u32[]{:S(2)}) copy-start(s32[16,2]{0,1:T(2,128)} %param.36) | copy-start | bytes 388
  75.7 116.4 %copy-start.4 = (bf16[16,4096]{1,0:T(8,128)(2,1)S(1)}, bf16[16,4096]{1,0:T(8,128)(2,1)}, u32[]{:S(2)}) copy-start(bf16[16,4096]{1,0:T(8,128)(2,1)} %param.33) | copy-start | bytes 393220
  75.7 117.4 %copy-start.8 = (f32[4096]{0:T(1024)S(1)}, f32[4096]{0:T(1024)}, u32[]{:S(2)}) copy-start(f32[4096]{0:T(1024)} %param.34) | copy-start | bytes 49156
  170.3 70.1 %all-gather.14.cloned.1.call-start = ((), (), s32[]{:S(2)}) async-start(), calls=%async_computation.7 | async-start | bytes 2949120 | tf_op jit(solution)/shard_map/all_gather | solution.py:118
  273.2 33.6 %copy-start.12 = (u32[32]{0:T(128)S(1)}, u32[32]{0:T(128)}, u32[]{:S(2)}) copy-start(u32[32]{0:T(128)} %constant.80) | copy-start | bytes 388
  305.4 2.7 collective-permute-start.1
  308.6 20.8 %copy-start.5 = (bf16[16,4096]{1,0:T(8,128)(2,1)S(1)}, bf16[16,4096]{1,0:T(8,128)(2,1)}, u32[]{:S(2)}) copy-start(bf16[16,4096]{1,0:T(8,128)(2,1)} %reduce-scatter.4.cloned.1.call-done) | copy-start | bytes 393220
  309.6 19.4 %all-to-all-start.1 = ((bf16[4,9,4096]{2,1,0:T(8,128)(2,1)}), bf16[4,9,4096]{2,1,0:T(8,128)(2,1)S(1)}, u32[]{:S(2)}, u32[]{:S(2)}) async-start(bf16[4,9,4096]{2,1,0:T(8,128)(2,1)} %reshape.358), calls=%async_computation.2 | async-start | bytes 1048576 | tf_op jit(solution)/shard_map/all_to_all | solution.py:126
Sparse Core Ops, SparseCore 0:
  13.5 26.0 all-gather.9
  42.1 23.4 all-gather.11
  67.5 93.0 all-gather.7
  170.4 21.6 reduce-scatter.3
  211.2 29.1 all-gather.13
where the time goes:
time: 340 us; the launch traced here: 337 us
  waiting for transfers between devices  194 us (57%)
  blocking collectives  47.6 us (14%)
  matrix products  38.8 us (11%)
  other arithmetic  19.8 us (6%)
  between operations  14.8 us (4%)
  local copies, waits for them, and re-layouts  12.6 us (4%)
  starting transfers between devices  8.59 us (3%)
    all_gather x1, waiting for transfers between devices, shards(): full_weight = lax.all_gather(out_weight, 'seq', axis=1, tiled=True)  85 us
    all_gather x2, waiting for transfers between devices, carried_in(): gathered = jax.tree.map(lambda a: lax.all_gather(a, axis), part)  42.7 us
    unnamed x1, blocking collectives  32.1 us
    all_gather x1, waiting for transfers between devices, shards(): piece = lax.all_gather(flat_rows, 'seq', axis=0, tiled=True)  29.3 us
    reduce_scatter x1, waiting for transfers between devices, shards(): lax.psum_scatter(jnp.dot(mixed, full_weight, preferred_element_type=jnp.f...  21.2 us
    dot_general x1, matrix products, shards(): jnp.dot(activated, down_weight[0], preferred_element_type=jnp.float32)  18.3 us
    all_to_all x1, blocking collectives, shards(): lax.all_to_all(outgoing, 'exp', split_axis=0, concat_axis=0, tiled=True)  15.5 us
    all_to_all x1, waiting for transfers between devices, shards(): lax.all_to_all(summed_out.reshape(arrived.shape), 'exp', split_axis=0, co...  14.7 us
  transfers between devices with their start and end apart: 8, of which 6 were waited for; matrix products, arithmetic and copies ran while one was open for 6% of the time, Pallas kernels for 0%

commit v1 on v0

v1 whole, which is shorter than its diff:
```python
import functools

import jax
import jax.numpy as jnp
from jax import lax
from jax.experimental import pallas as pl
from jax.experimental.pallas import tpu as pltpu
from jax.sharding import PartitionSpec as P

KCONV = 4
MESH = pl.DeviceIdType.MESH
VMEM_LIMIT = 58 * 2**20


def from_behind(block, axis, distance):
    devices = range(lax.axis_size(axis))
    route = [(i - distance, i) for i in devices if i - distance in devices]
    return lax.ppermute(block, axis, route)


def place():
    me = lax.axis_index("seq")
    z = lax.axis_index("exp")
    core = lax.rem(me, 2)
    return me, z, core, lax.div(me, 2)


def greet(peers):
    barrier = pltpu.get_barrier_semaphore()
    for peer in peers:
        pl.semaphore_signal(barrier, inc=1, device_id=peer, device_id_type=MESH)
    pl.semaphore_wait(barrier, len(peers))


def push(src, dst, send_sem, recv_sem, peer):
    return pltpu.make_async_remote_copy(
        src_ref=src,
        dst_ref=dst,
        send_sem=send_sem,
        recv_sem=recv_sem,
        device_id=peer,
        device_id_type=MESH,
    )


def mixer_kernel(
    n, conv_ref, delta_ref, in_ref, out_coef_ref, rate_ref, skip_ref, gate_ref, out_ref,
    own_end, own_sum, ends, sums, start, s_end, r_end, s_sum, r_sum,
):
    me, z, core, chip = place()
    groups, states, span = own_end.shape
    parts = span // 128
    blocks = conv_ref.shape[0] // 16

    barrier = pltpu.get_barrier_semaphore()
    for d in range(1, n):
        peer = (lax.rem(me + d, n), z)
        pl.semaphore_signal(barrier, inc=1, device_id=peer, device_id_type=MESH)

    def copies(g, d):
        peer = (lax.rem(me + d, n), z)
        i = d - 1
        return (
            push(own_end.at[g], ends.at[g, i], s_end.at[g, i], r_end.at[g, i], peer),
            push(own_sum.at[g], sums.at[g, i], s_sum.at[g, i], r_sum.at[g, i], peer),
        )

    def walk(g, begin, emit):

        def block(b, carry):
            base = pl.multiple_of(b * 16, 16)
            tokens = pl.ds(base, 16)
            result = []
            for j in range(parts):
                lanes = slice(g * span + j * 128, g * span + (j + 1) * 128)
                delta = delta_ref[tokens, lanes]
                value = conv_ref[tokens, lanes]
                rate = -rate_ref[:, lanes]
                state = carry[j]
                rows = []
                for i in range(16):
                    retain = jnp.exp(delta[i : i + 1] * rate)
                    goal = in_ref[base + i] * value[i : i + 1]
                    state = goal + retain * (state - goal)
                    if emit:
                        rows.append(jnp.sum(out_coef_ref[base + i] * state, axis=0, keepdims=True))
                result.append(state)
                if emit:
                    scan_out = jnp.concatenate(rows, axis=0)
                    gate = gate_ref[tokens, lanes].astype(jnp.float32)
                    mixed = (scan_out + skip_ref[:, lanes] * value) * jax.nn.silu(gate)
                    out_ref[tokens, lanes] = mixed.astype(jnp.bfloat16)
            return tuple(result)

        return lax.fori_loop(0, blocks, block, begin)

    for g in range(groups):
        last = walk(g, (jnp.zeros((states, 128), jnp.float32),) * parts, False)
        for j in range(parts):
            own_end[g, :, j * 128 : (j + 1) * 128] = last[j].astype(jnp.bfloat16)
        own_sum[g] = jnp.sum(delta_ref[:, g * span : (g + 1) * span], axis=0, keepdims=True)
        if g == 0:
            pl.semaphore_wait(barrier, n - 1)
        for d in range(1, n):

            @pl.when(me + d < n)
            def _():
                for copy in copies(g, d):
                    copy.start()

    for g in range(groups):
        start[...] = jnp.zeros_like(start)
        for d in range(n - 1, 0, -1):

            @pl.when(me - d >= 0)
            def _():
                for copy in copies(g, d):
                    copy.wait_recv()
                decay = jnp.exp(-sums[g, d - 1] * rate_ref[:, g * span : (g + 1) * span])
                start[...] = decay * start[...] + ends[g, d - 1].astype(jnp.float32)

        walk(g, tuple(start[:, j * 128 : (j + 1) * 128] for j in range(parts)), True)

    for g in range(groups):
        for d in range(1, n):

            @pl.when(me + d < n)
            def _():
                for copy in copies(g, d):
                    copy.wait_send()


def mix(n, convolved, delta, input_coef, output_coef, decay_rate, skip_gain, gate_input):
    states, width = decay_rate.shape
    length = convolved.shape[0]
    span = 512
    groups = width // span
    vmem = pl.BlockSpec(memory_space=pltpu.VMEM)
    sems = pltpu.SemaphoreType.DMA((groups, n - 1))

    def spread(coef):
        return jnp.broadcast_to(coef.astype(jnp.float32)[:, :, None], (length, states, 128))

    return pl.pallas_call(
        functools.partial(mixer_kernel, n),
        out_shape=jax.ShapeDtypeStruct((length, width), jnp.bfloat16),
        in_specs=[vmem] * 7,
        out_specs=vmem,
        scratch_shapes=[
            pltpu.VMEM((groups, states, span), jnp.bfloat16),
            pltpu.VMEM((groups, 1, span), jnp.float32),
            pltpu.VMEM((groups, n - 1, states, span), jnp.bfloat16),
            pltpu.VMEM((groups, n - 1, 1, span), jnp.float32),
            pltpu.VMEM((states, span), jnp.float32),
            sems,
            sems,
            sems,
            sems,
        ],
        compiler_params=pltpu.CompilerParams(
            collective_id=0, has_side_effects=True, vmem_limit_bytes=VMEM_LIMIT
        ),
    )(
        convolved,
        delta,
        spread(input_coef),
        spread(output_coef),
        decay_rate,
        skip_gain[None, :],
        gate_input,
    )


def project_kernel(
    n, e, mixed_ref, weight_ref, out_ref, gath, part, zrecv, total, orecv,
    s_a, r_a, s_b, r_b, s_z, r_z, s_o, r_o,
):
    me, z, core, chip = place()
    nc = n // 2
    length, width = mixed_ref.shape
    cols = weight_ref.shape[1]
    rows = length // e
    partner = (me + 1 - 2 * core, z)
    greet(
        [(lax.rem(me + d, n), z) for d in range(1, n)]
        + [(me, lax.rem(z + d, e)) for d in range(1, e)]
    )

    across = []
    for d in range(1, nc):
        peer = (lax.rem(chip + d, nc) * 2 + core, z)
        across.append(push(mixed_ref, gath.at[me], s_a.at[d - 1], r_a.at[d - 1], peer))
        across[-1].start()
    beside = [push(mixed_ref, gath.at[me], s_b.at[0], r_b.at[0], partner)]
    beside[0].start()
    gath[me] = mixed_ref[...]

    along = []
    sent = []
    for d in range(nc):
        k = lax.rem(chip - d + nc, nc)
        if d + 1 < nc:
            across[d].wait_recv()
            src = lax.rem(chip - d - 1 + nc, nc) * 2 + core
            beside.append(push(gath.at[src], gath.at[src], s_b.at[d + 1], r_b.at[d + 1], partner))
            beside[-1].start()
        beside[d].wait_recv()
        block = gath[pl.ds(2 * k, 2)].reshape(2 * length, width)
        term = jnp.dot(block, weight_ref[...], preferred_element_type=jnp.float32)
        term = term.astype(jnp.bfloat16)
        for c in range(2):
            for q in range(e):
                begin = (c * e + q) * rows
                part[q, 2 * k + c] = term[begin : begin + rows]
        group = []
        for dz in range(1, e):
            q = lax.rem(z + dz, e)
            pair = pl.ds(2 * k, 2)
            group.append(
                push(part.at[q, pair], zrecv.at[z, pair], s_z.at[d, dz - 1], r_z.at[d, dz - 1], (me, q))
            )
            group[-1].start()
        along.append(group)

    for d in range(nc):
        k = lax.rem(chip - d + nc, nc)
        pair = pl.ds(2 * k, 2)
        acc = part[z, pair].astype(jnp.float32)
        for dz in range(1, e):
            along[d][dz - 1].wait_recv()
            acc = acc + zrecv[lax.rem(z - dz + e, e), pair].astype(jnp.float32)
        total[pair] = acc.astype(jnp.bfloat16)
        for c in ((0, 1) if d else (1,)):
            other = lax.rem(core + c, 2)
            s = 2 * k + other
            gap = lax.rem(me - s + n, n) - 1
            sent.append(push(total.at[s], orecv.at[me], s_o.at[gap], r_o.at[gap], (s, z)))
            sent[-1].start()
    orecv[me] = total[me]
    for g in range(n - 1):
        push(total.at[0], orecv.at[0], s_o.at[g], r_o.at[g], partner).wait_recv()
    for j in range(n):
        out_ref[:, j * cols : (j + 1) * cols] = orecv[j].astype(jnp.float32)
    for copy in across + beside + sum(along, []) + sent:
        copy.wait_send()


def project(n, e, mixed, out_weight):
    length, width = mixed.shape
    cols = out_weight.shape[1]
    rows = length // e
    vmem = pl.BlockSpec(memory_space=pltpu.VMEM)
    dma = pltpu.SemaphoreType.DMA
    nc = n // 2
    return pl.pallas_call(
        functools.partial(project_kernel, n, e),
        out_shape=jax.ShapeDtypeStruct((rows, n * cols), jnp.float32),
        in_specs=[vmem] * 2,
        out_specs=vmem,
        scratch_shapes=[
            pltpu.VMEM((n, length, width), jnp.bfloat16),
            pltpu.VMEM((e, n, rows, cols), jnp.bfloat16),
            pltpu.VMEM((e, n, rows, cols), jnp.bfloat16),
            pltpu.VMEM((n, rows, cols), jnp.bfloat16),
            pltpu.VMEM((n, rows, cols), jnp.bfloat16),
            dma((nc - 1,)),
            dma((nc - 1,)),
            dma((nc,)),
            dma((nc,)),
            dma((nc, e - 1)),
            dma((nc, e - 1)),
            dma((n - 1,)),
            dma((n - 1,)),
        ],
        compiler_params=pltpu.CompilerParams(
            collective_id=1, has_side_effects=True, vmem_limit_bytes=VMEM_LIMIT
        ),
        cost_estimate=pl.CostEstimate(
            flops=2 * n * length * width * cols, bytes_accessed=2 * width * cols, transcendentals=0
        ),
    )(mixed, out_weight)


def expert_kernel(
    n, e, tile, chunk,
    og_ref, pack_ref, unpack_ref, gate_hbm, up_hbm, down_hbm, out_ref,
    gate, up, down, disp, xs, act, ysend, yrecv, red, rbuf, ret, home,
    s_w, s_d, r_d, s_a, r_a, s_b, r_b, s_y, r_y, s_r, r_r, s_h, r_h,
):
    me, z, core, chip = place()
    nc = n // 2
    half = xs.shape[3]
    slots = xs.shape[2]
    hidden = act.shape[1]
    depth = 2 * half
    capp = og_ref.shape[1]
    other = 1 - core
    mate = me + 1 - 2 * core
    partner = (mate, z)

    loads = [
        pltpu.make_async_copy(gate_hbm.at[0], gate, s_w.at[0]),
        pltpu.make_async_copy(up_hbm.at[0], up, s_w.at[1]),
        pltpu.make_async_copy(down_hbm.at[0], down, s_w.at[2]),
    ]
    for load in loads:
        load.start()

    greet(
        [partner]
        + [(lax.rem(chip + d, nc) * 2 + core, z) for d in range(1, nc)]
        + [(s, lax.rem(z + d, e)) for d in range(1, e) for s in (me, mate)]
    )

    chunks = half // chunk

    def lanes(which, i):
        return pl.ds(pl.multiple_of(which * half + i * chunk, 128), chunk)

    routed = []
    for p in range(chunks):
        group = []
        for dz in range(e):
            q = lax.rem(z + dz, e)
            for dc in range(2):
                if dz == 0 and dc == 0:
                    continue
                s, c = ((me, core), (mate, other))[dc]
                i = 2 * dz + dc - 1
                src = og_ref.at[q, :, lanes(c, p)]
                group.append(push(src, disp.at[p, z, core], s_d.at[p, i], r_d.at[p, i], (s, q)))
                group[-1].start()
        disp[p, z, core] = og_ref[z, :, lanes(core, p)]
        routed.append(group)

    across = []
    beside = []

    def relay(p):
        for d in range(1, nc):
            across[p][d - 1].wait_recv()
            src = xs.at[lax.rem(chip - d + nc, nc), core, :, p * chunk : (p + 1) * chunk]
            beside[p].append(push(src, src, s_b.at[p, d], r_b.at[p, d], partner))
            beside[p][-1].start()

    for p in range(chunks):
        for copy in routed[p]:
            copy.wait_recv()
        xs[chip, core, :, p * chunk : (p + 1) * chunk] = jnp.dot(
            pack_ref[...], disp[p].reshape(2 * e * capp, chunk), preferred_element_type=jnp.float32
        ).astype(jnp.bfloat16)
        mine = xs.at[chip, core, :, p * chunk : (p + 1) * chunk]
        group = []
        for d in range(1, nc):
            peer = (lax.rem(chip + d, nc) * 2 + core, z)
            group.append(push(mine, mine, s_a.at[p, d - 1], r_a.at[p, d - 1], peer))
            group[-1].start()
        across.append(group)
        beside.append([push(mine, mine, s_b.at[p, 0], r_b.at[p, 0], partner)])
        beside[p][0].start()
        if p:
            relay(p - 1)
    relay(chunks - 1)
    for copy in sum(beside, []):
        copy.wait_recv()
    loads[0].wait()
    loads[1].wait()

    def up_step(f, carry):
        at = pl.ds(pl.multiple_of(f * tile, 128), tile)
        x0 = xs[:, 0].reshape(nc * slots, half)
        x1 = xs[:, 1].reshape(nc * slots, half)
        g = jnp.dot(x0, gate[0:half, at], preferred_element_type=jnp.float32)
        g = g + jnp.dot(x1, gate[half:depth, at], preferred_element_type=jnp.float32)
        u = jnp.dot(x0, up[0:half, at], preferred_element_type=jnp.float32)
        u = u + jnp.dot(x1, up[half:depth, at], preferred_element_type=jnp.float32)
        act[:, at] = (jax.nn.silu(g) * u).astype(jnp.bfloat16)
        return carry

    lax.fori_loop(0, hidden // tile, up_step, 0)
    loads[2].wait()

    def down_chunk(which, i):
        at = pl.ds(pl.multiple_of(which * half + i * chunk, 128), chunk)
        return jnp.dot(act[...], down[:, at], preferred_element_type=jnp.float32)

    paired = []
    for i in range(chunks):
        ysend[i] = down_chunk(other, i).astype(jnp.bfloat16)
        paired.append(push(ysend.at[i], yrecv.at[i], s_y.at[i], r_y.at[i], partner))
        paired[-1].start()
    summed = []
    back = []

    def settle(i):
        acc = red[i, chip].astype(jnp.float32)
        for d in range(1, nc):
            summed[i][d - 1].wait_recv()
            acc = acc + rbuf[i, d - 1].astype(jnp.float32)
        spread = jnp.dot(
            unpack_ref[...], acc.astype(jnp.bfloat16), preferred_element_type=jnp.float32
        ).astype(jnp.bfloat16)
        ret[i] = spread.reshape(e, 2, capp, chunk)
        for dz in range(e):
            q = lax.rem(z + dz, e)
            for dc in range(2):
                if dz == 0 and dc == 0:
                    continue
                s, c = ((me, core), (mate, other))[dc]
                k = 2 * dz + dc - 1
                dst = home.at[z, :, lanes(core, i)]
                back.append(push(ret.at[i, q, c], dst, s_h.at[i, k], r_h.at[i, k], (s, q)))
                back[-1].start()
        home[z, :, lanes(core, i)] = ret[i, z, core]

    for i in range(chunks):
        y = down_chunk(core, i)
        paired[i].wait_recv()
        y = (y + yrecv[i].astype(jnp.float32)).astype(jnp.bfloat16)
        red[i] = y.reshape(nc, slots, chunk)
        group = []
        for d in range(1, nc):
            k = lax.rem(chip + d, nc)
            group.append(
                push(red.at[i, k], rbuf.at[i, d - 1], s_r.at[i, d - 1], r_r.at[i, d - 1], (k * 2 + core, z))
            )
            group[-1].start()
        summed.append(group)
    for i in range(chunks):
        settle(i)

    for copy in back:
        copy.wait_recv()
    out_ref[...] = home[...]
    for copy in sum(routed + across + beside + summed, []) + paired + back:
        copy.wait_send()


def experts_apply(n, e, cap, outgoing, gate_weight, up_weight, down_weight):
    capp, width = outgoing.shape[1:]
    hidden = gate_weight.shape[2]
    nc = n // 2
    half = width // 2
    used = 2 * e * cap
    slots = -(-used // 16) * 16
    tile = 256 if hidden % 256 == 0 else 128
    chunk = 512
    chunks = half // chunk
    spots = jnp.arange(2 * e * capp)
    inside = spots % capp
    goal = jnp.where(inside < cap, (spots // capp) * cap + inside, -1)
    pack = (jnp.arange(slots)[:, None] == goal[None, :]).astype(jnp.bfloat16)
    vmem = pl.BlockSpec(memory_space=pltpu.VMEM)
    hbm = pl.BlockSpec(memory_space=pl.ANY)
    dma = pltpu.SemaphoreType.DMA
    bf = jnp.bfloat16
    return pl.pallas_call(
        functools.partial(expert_kernel, n, e, tile, chunk),
        out_shape=jax.ShapeDtypeStruct((e, capp, width), bf),
        in_specs=[vmem] * 3 + [hbm] * 3,
        out_specs=vmem,
        scratch_shapes=[
            pltpu.VMEM((width, hidden), bf),
            pltpu.VMEM((width, hidden), bf),
            pltpu.VMEM((hidden, width), bf),
            pltpu.VMEM((chunks, e, 2, capp, chunk), bf),
            pltpu.VMEM((nc, 2, slots, half), bf),
            pltpu.VMEM((nc * slots, hidden), bf),
            pltpu.VMEM((chunks, nc * slots, chunk), bf),
            pltpu.VMEM((chunks, nc * slots, chunk), bf),
            pltpu.VMEM((chunks, nc, slots, chunk), bf),
            pltpu.VMEM((chunks, nc - 1, slots, chunk), bf),
            pltpu.VMEM((chunks, e, 2, capp, chunk), bf),
            pltpu.VMEM((e, capp, width), bf),
            dma((3,)),
            dma((chunks, 2 * e - 1)),
            dma((chunks, 2 * e - 1)),
            dma((chunks, nc - 1)),
            dma((chunks, nc - 1)),
            dma((chunks, nc)),
            dma((chunks, nc)),
            dma((chunks,)),
            dma((chunks,)),
            dma((chunks, nc - 1)),
            dma((chunks, nc - 1)),
            dma((chunks, 2 * e - 1)),
            dma((chunks, 2 * e - 1)),
        ],
        compiler_params=pltpu.CompilerParams(
            collective_id=2, has_side_effects=True, vmem_limit_bytes=VMEM_LIMIT
        ),
        cost_estimate=pl.CostEstimate(
            flops=6 * nc * slots * width * hidden,
            bytes_accessed=6 * width * hidden,
            transcendentals=nc * slots * hidden,
        ),
    )(outgoing, pack, pack.T, gate_weight, up_weight, down_weight)


def shards(
    n,
    e,
    mixer_input,
    gate_input,
    delta_raw,
    input_coef,
    output_coef,
    decay_rate,
    conv_weight,
    conv_bias,
    skip_gain,
    out_weight,
    residual,
    norm_gain,
    router_weight,
    expert_ids,
    gate_weight,
    up_weight,
    down_weight,
):
    length = mixer_input.shape[0]
    width = mixer_input.shape[1]
    tail = mixer_input[length - (KCONV - 1) :]
    before = from_behind(tail, "seq", 1)
    padded = jnp.concatenate([before, mixer_input], axis=0).astype(jnp.float32)
    summed = jnp.broadcast_to(conv_bias[None, :], (length, width))
    for offset in range(KCONV):
        summed = summed + conv_weight[offset][None, :] * padded[offset : offset + length]
    convolved = jax.nn.silu(summed)
    delta = jax.nn.softplus(delta_raw.astype(jnp.float32))
    mixed = mix(
        n, convolved, delta, input_coef, output_coef, decay_rate, skip_gain, gate_input
    )
    rows = residual.shape[0]
    model_width = residual.shape[1]
    projected = project(n, e, mixed, out_weight)
    hidden_state = residual.astype(jnp.float32) + projected
    scale = lax.rsqrt(jnp.mean(hidden_state * hidden_state, axis=1, keepdims=True) + 1e-06)
    normed = (hidden_state * scale * norm_gain[None, :]).astype(jnp.bfloat16)
    capacity = 2 * rows // e + 1
    capp = -(-capacity // 16) * 16
    logits = jnp.dot(normed, router_weight, preferred_element_type=jnp.float32)
    expert_range = jnp.arange(e, dtype=jnp.int32)
    matches = expert_ids[:, :, None] == expert_range[None, None, :]
    chosen = jnp.sum(jnp.where(matches, logits[:, None, :], 0.0), axis=2)
    first = jax.nn.sigmoid(chosen[:, 0] - chosen[:, 1])
    flat_ids = expert_ids.reshape(-1)
    onehot = (flat_ids[:, None] == expert_range[None, :]).astype(jnp.int32)
    rank = jnp.sum((jnp.cumsum(onehot, axis=0) - onehot) * onehot, axis=1)
    target = flat_ids * capp + rank
    slot_range = jnp.arange(e * capp, dtype=jnp.int32)
    placing = (slot_range[:, None, None] == target.reshape(rows, 2)[None]).astype(jnp.bfloat16)
    outgoing = (
        jnp.dot(placing[:, :, 0] + placing[:, :, 1], normed, preferred_element_type=jnp.float32)
        .astype(jnp.bfloat16)
        .reshape(e, capp, model_width)
    )
    returned = experts_apply(n, e, capacity, outgoing, gate_weight, up_weight, down_weight)
    flat_returned = returned.reshape(-1, model_width)
    picked = [
        jnp.einsum("sa,sd->ad", placing[:, :, k], flat_returned, preferred_element_type=jnp.float32)
        for k in range(2)
    ]
    moe_out = first[:, None] * picked[0] + (1.0 - first)[:, None] * picked[1]
    final = (hidden_state + moe_out).astype(jnp.bfloat16)
    return (mixed, final)


def solution(mesh):
    return jax.shard_map(
        functools.partial(shards, mesh.shape["seq"], mesh.shape["exp"]),
        mesh=mesh,
        in_specs=(
            P("seq", "exp"),
            P("seq", "exp"),
            P("seq", "exp"),
            P("seq", None),
            P("seq", None),
            P(None, "exp"),
            P(None, "exp"),
            P("exp"),
            P("exp"),
            P("exp", "seq"),
            P(("seq", "exp"), None),
            P(),
            P(),
            P(("seq", "exp"), None),
            P("exp", None, "seq"),
            P("exp", None, "seq"),
            P("exp", "seq", None),
        ),
        out_specs=(P("seq", "exp"), P(("seq", "exp"), None)),
        check_vma=False,
    )
```

time: 340 us -> 138 us (0.41)
  waiting for transfers between devices: 194 us -> 0.01 us
  Pallas kernels: 0 us -> 113 us
  blocking collectives: 47.6 us -> 0 us
  matrix products: 38.8 us -> 4.4 us
  between operations: 14.8 us -> 0.79 us
  other arithmetic: 19.8 us -> 9.5 us
  starting transfers between devices: 8.59 us -> 2.36 us
  local copies, waits for them, and re-layouts: 12.6 us -> 7.07 us
    all_gather x4 -> x0, waiting for transfers between devices: 157 us -> none  [the longest x1 85 us: shards(): full_weight = lax.all_gather(out_weight, 'seq', axis=1, tiled=True)]
    pallas_call x0 -> x3, Pallas kernels: none -> 113 us  [the longest x1 65.4 us: experts_apply(): pl.pallas_call(functools.partial(expert_kernel, n, e, tile, chunk), out_s...]
    dot_general x5 -> x3, matrix products: 38.7 us -> 4.25 us  [the longest x2 3.12 us: shards(): jnp.einsum('sa,sd->ad', placing[:, :, k], flat_returned, preferred_elemen...]
    unnamed x1 -> x0, blocking collectives: 32.1 us -> none
    reduce_scatter x1 -> x0, waiting for transfers between devices: 21.2 us -> none  [shards(): lax.psum_scatter(jnp.dot(mixed, full_weight, preferred_element_type=jnp.f...]
    all_to_all x1 -> x0, blocking collectives: 15.5 us -> none  [shards(): lax.all_to_all(outgoing, 'exp', split_axis=0, concat_axis=0, tiled=True)]
    all_to_all x1 -> x0, waiting for transfers between devices: 14.7 us -> none  [shards(): lax.all_to_all(summed_out.reshape(arrived.shape), 'exp', split_axis=0, co...]
    reduce_sum x24 -> x0, other arithmetic: 6.57 us -> none  [advance(): return (carry, jnp.sum(output_row[:, None] * carry, axis=0))]
  transfers between devices with their start and end apart: 8 -> 1, of which waited for: 6 -> 0; matrix products, arithmetic and copies ran while one was open for 6% -> 6% of each run, Pallas kernels for 0% -> 0%
where the time goes in v1:
time: 138 us
  Pallas kernels  113 us (82%)
  other arithmetic  9.5 us (7%)
  local copies, waits for them, and re-layouts  7.07 us (5%)
  matrix products  4.4 us (3%)
  starting transfers between devices  2.36 us (2%)
    pallas_call x1, Pallas kernels, experts_apply(): pl.pallas_call(functools.partial(expert_kernel, n, e, tile, chunk), out_s...  65.4 us
    pallas_call x1, Pallas kernels, project(): pl.pallas_call(functools.partial(project_kernel, n, e), out_shape=jax.Sha...  34 us
    pallas_call x1, Pallas kernels, mix(): pl.pallas_call(functools.partial(mixer_kernel, n), out_shape=jax.ShapeDty...  14.1 us
    dot_general x2, matrix products, shards(): jnp.einsum('sa,sd->ad', placing[:, :, k], flat_returned, preferred_elemen...  3.12 us
  transfers between devices with their start and end apart: 1, of which 0 were waited for; matrix products, arithmetic and copies ran while one was open for 6% of the time, Pallas kernels for 0%

profile of v1, /device:TPU:0, one launch (start us, length us, event | category | flops | bytes accessed | tf_op | source)
XLA Modules:
  0.0 137.6 jit_solution(15238199734667056896)
XLA Ops:
  0.6 0.0 copy-start
  0.6 0.0 copy-start.5
  0.7 0.0 copy-start.2
  0.7 0.0 copy-start.4
  0.7 0.8 slice.46
  1.5 2.4 %collective-permute-start = (bf16[3,2048]{1,0:T(4,128)(2,1)S(1)}, bf16[3,2048]{1,0:T(4,128)(2,1)S(1)}, u32[]{:S(2)}, u32[]{:S(2)}) collective-permute-start(bf16[3,2048]{1,0:T(4,128)(2,1)S(1)} %slice.46), channel_id=1, source_target_pairs={{0,4},{4,8},{8,12},{12,16},{16,20},{20,24},{24,28},{1,5},{5,9},{9,... | collective-permute-start | bytes 36872 | tf_op jit(solution)/shard_map/ppermute | solution.py:18
  3.9 0.7 fusion.11.unpack_ref
  4.6 0.6 fusion.12.pack_ref
  5.2 0.9 fusion.20
  6.1 2.1 %compare_select_fusion.delta_ref = f32[64,2048]{1,0:T(8,128)} fusion(bf16[64,2048]{1,0:T(8,128)(2,1)} %param.19), kind=kLoop, calls=%fused_computation.6 | loop fusion | flops 917504 | bytes 786432 | tf_op jit(solution)/shard_map/jit(softplus)/select_n | solution.py:530
  8.2 0.8 copy.42
  8.9 0.1 eq.67
  9.0 0.1 fusion.13
  9.1 0.1 reduce_window_sum.11
  9.2 0.2 select_reduce_fusion
  9.3 0.1 reduce_sum.32
  9.4 0.1 copy.43
  9.5 0.7 multiply_add_fusion
  10.2 0.1 iota_compare_fusion.3
  10.3 0.8 copy.40
  11.1 0.8 copy.41
  11.8 0.0 collective-permute-done
  11.8 1.0 maximum_convert_fusion
  12.9 1.8 %divide_multiply_fusion.conv_ref = f32[64,2048]{1,0:T(8,128)} fusion(f32[67,2048]{1,0:T(8,128)S(1)} %maximum_convert_fusion, f32[2048]{0:T(1024)S(1)} %bitcast.29, f32[2048]{0:T(1024)S(1)} %bitcast.30, f32[2048]{0:T(1024)S(1)} %bitcast.28, f32[2048]{0:T(1024)S(1)} %bitcast.27, f32[2048]{0:T(1024)} %param.24), kind=kLoop, calls=%fused_computation.21 | loop fusion | flops 1572864 | bytes 2662400 | tf_op jit(solution)/shard_map/jit(silu)/mul | solution.py:529
  14.7 1.0 broadcast_in_dim.18.in_ref
  15.7 1.0 broadcast_in_dim.19.out_coef_ref
  16.7 14.1 %shard_map.176.mixed_ref = bf16[64,2048]{1,0:T(8,128)(2,1)} custom-call(f32[64,2048]{1,0:T(8,128)} %divide_multiply_fusion.conv_ref, f32[64,2048]{1,0:T(8,128)} %compare_select_fusion.delta_ref, f32[64,16,128]{2,1,0:T(8,128)} %broadcast_in_dim.18.in_ref, f32[64,16,128]{2,1,0:T(8,128)} %broadcast_in_dim.19.out_coef_ref, f32[16,2048]{1,0:T(8,128)} %rate_ref.1, ...), custom_call_target="tpu_custom_call" | custom-call | tf_op jit(solution)/shard_map/pallas_call | solution.py:144
  30.8 34.0 %shard_map.177 = f32[16,4096]{1,0:T(8,128)} custom-call(bf16[64,2048]{1,0:T(8,128)(2,1)} %shard_map.176.mixed_ref, bf16[2048,512]{1,0:T(8,128)(2,1)} %weight_ref.1), custom_call_target="tpu_custom_call" | custom-call | flops 1073741824 | bytes 2097152 | tf_op jit(solution)/shard_map/pallas_call | solution.py:255
  64.9 0.0 copy-done.2
  64.9 1.1 multiply_reduce_fusion
  66.0 0.0 copy-done.4
  66.0 1.0 multiply_convert_fusion
  67.0 1.1 convolution_convert_fusion
  68.2 0.0 copy-done
  68.2 0.1 fusion.21
  68.3 0.0 copy-done.5
  68.4 0.0 copy-start.1
  68.4 0.0 copy-start.3
  68.4 65.4 %shard_map.178 = bf16[4,16,4096]{2,1,0:T(8,128)(2,1)} custom-call(bf16[4,16,4096]{2,1,0:T(8,128)(2,1)} %bitcast.26, bf16[80,128]{1,0:T(8,128)(2,1)} %fusion.12.pack_ref, bf16[128,80]{1,0:T(8,128)(2,1)} %fusion.11.unpack_ref, bf16[1,4096,1536]{2,1,0:T(8,128)(2,1)} %gate_hbm.1, bf16[1,4096,1536]{2,1,0:T(8,128)(2,1)} %up_hbm.1, bf16[1,1536,4096]{2,1,0:T(8,128)(2,1)} %down_hbm.1), custom_call_target="tpu_custom_call" | custom-call | flops 12079595520 | bytes 37748736 | tf_op jit(solution)/shard_map/pallas_call | solution.py:457
  133.8 1.2 convolution_multiply_fusion.1
  135.0 0.0 copy-done.1
  135.0 1.9 %fusion.2 = bf16[16,4096]{1,0:T(8,128)(2,1)} fusion(f32[16,4096]{1,0:T(8,128)S(1)} %convolution_multiply_fusion.1, bf16[64,4096]{1,0:T(8,128)(2,1)} %bitcast.25, f32[16]{0:T(128)S(1)} %get-tuple-element.2, f32[16,4096]{1,0:T(8,128)S(1)} %copy-done.1, bf16[16,4096]{1,0:T(8,128)(2,1)S(1)} %copy-done.2, pred[64,16,2]{0,1,2:T(8,128)(4,1)S(1)} %get-tuple-element.8), kind=kOutput, calls=%fused_computation.5 | convolution fusion | flops 8781824 | bytes 1313280 | tf_op jit(solution)/shard_map/sa,sd->ad/dot_general | solution.py:561
  136.9 0.0 copy-done.3
  136.9 0.7 copy.45
  (4 shorter events, 0.1 us)
Async XLA Ops:
  0.6 67.5 %copy-start = (bf16[4096,4]{0,1:T(4,128)(2,1)S(1)}, bf16[4096,4]{0,1:T(4,128)(2,1)}, u32[]{:S(2)}) copy-start(bf16[4096,4]{0,1:T(4,128)(2,1)} %param.29) | copy-start | bytes 98308
  0.6 67.7 %copy-start.5 = (s32[16,2]{0,1:T(2,128)S(1)}, s32[16,2]{0,1:T(2,128)}, u32[]{:S(2)}) copy-start(s32[16,2]{0,1:T(2,128)} %param.30) | copy-start | bytes 388
  0.7 64.2 %copy-start.2 = (bf16[16,4096]{1,0:T(8,128)(2,1)S(1)}, bf16[16,4096]{1,0:T(8,128)(2,1)}, u32[]{:S(2)}) copy-start(bf16[16,4096]{1,0:T(8,128)(2,1)} %param.27) | copy-start | bytes 393220
  0.7 65.3 %copy-start.4 = (f32[4096]{0:T(1024)S(1)}, f32[4096]{0:T(1024)}, u32[]{:S(2)}) copy-start(f32[4096]{0:T(1024)} %param.28) | copy-start | bytes 49156
  1.5 10.3 %collective-permute-start = (bf16[3,2048]{1,0:T(4,128)(2,1)S(1)}, bf16[3,2048]{1,0:T(4,128)(2,1)S(1)}, u32[]{:S(2)}, u32[]{:S(2)}) collective-permute-start(bf16[3,2048]{1,0:T(4,128)(2,1)S(1)} %slice.46), channel_id=1, source_target_pairs={{0,4},{4,8},{8,12},{12,16},{16,20},{20,24},{24,28},{1,5},{5,9},{9,... | collective-permute-start | bytes 36872 | tf_op jit(solution)/shard_map/ppermute | solution.py:18
  68.4 66.6 %copy-start.1 = (f32[16,4096]{1,0:T(8,128)S(1)}, f32[16,4096]{1,0:T(8,128)}, u32[]{:S(2)}) copy-start(f32[16,4096]{1,0:T(8,128)} %shard_map.177) | copy-start | bytes 786436
  68.4 68.5 %copy-start.3 = (bf16[64,2048]{1,0:T(8,128)(2,1)S(1)}, bf16[64,2048]{1,0:T(8,128)(2,1)}, u32[]{:S(2)}) copy-start(bf16[64,2048]{1,0:T(8,128)(2,1)} %shard_map.176.mixed_ref) | copy-start | bytes 786436
